TPU v7x, 256 devices: a whole 4x4x8 slice. The times are simulated.
256 devices in a mesh: row: 8 (over y_lo, x), col: 32 (over y_hi, z, core).
Axes of the slice: x: 4, y: 4 (y_hi: 2, y_lo: 2; y = y_hi * 2 + y_lo), z: 8, core: 2. Of those that a mesh axis runs over, the one named last changes fastest.
Arguments:
- inputs: bfloat16 [256, 14336], P('col', 'row'), may hold values from -6 to 6
- out_grad: bfloat16 [256, 14336], P('col', 'row'), may hold values from -6 to 6
- w_in: bfloat16 [14336, 29696], P('row', 'col'), may hold values from -0.046875 to 0.046875
- w_out: bfloat16 [29696, 14336], P('col', 'row'), may hold values from -0.03125 to 0.03125
Outputs:
- in_grad: bfloat16 [256, 14336], P('col', 'row')
- w_in_grad: bfloat16 [14336, 29696], P('row', 'col')
- w_out_grad: bfloat16 [29696, 14336], P('col', 'row')
All inputs are finite; a program needn't handle non-finite values.
Results may differ from a plain program's by a relative error of at most 0.022.
Values may be sent and summed in bfloat16 or wider, within the bound.
A program may use at most 64 MiB of HBM per device.

v0:
```python
import math

import jax
import jax.numpy as jnp
from jax import lax
from jax.sharding import PartitionSpec as P


def activate(pre, back):
    cdf = 0.5 * (1.0 + jax.scipy.special.erf(pre / math.sqrt(2.0)))
    hidden = (pre * cdf).astype(jnp.bfloat16)
    slope = cdf + pre * jnp.exp(-0.5 * pre * pre) / math.sqrt(2.0 * math.pi)
    pre_grad = (back * slope).astype(jnp.bfloat16)
    return (hidden, pre_grad)


def on_device(inputs, out_grad, w_in, w_out):
    full_in, full_grad = (
        lax.all_gather(inputs, "col", axis=0, tiled=True),
        lax.all_gather(out_grad, "col", axis=0, tiled=True),
    )
    pre_part = jnp.dot(full_in, w_in, preferred_element_type=jnp.float32)
    back_part = lax.dot_general(
        full_grad, w_out, (((1,), (1,)), ((), ())), preferred_element_type=jnp.float32
    )
    pre, back = lax.psum((pre_part, back_part), "row")
    hidden, pre_grad = activate(pre, back)
    w_out_grad = lax.dot_general(
        hidden, full_grad, (((0,), (0,)), ((), ())), preferred_element_type=jnp.float32
    ).astype(jnp.bfloat16)
    w_in_grad = lax.dot_general(
        full_in, pre_grad, (((0,), (0,)), ((), ())), preferred_element_type=jnp.float32
    ).astype(jnp.bfloat16)
    in_grad = lax.psum_scatter(
        lax.dot_general(
            pre_grad, w_in, (((1,), (1,)), ((), ())), preferred_element_type=jnp.float32
        ).astype(jnp.bfloat16),
        "col",
        scatter_dimension=0,
        tiled=True,
    )
    return (in_grad, w_in_grad, w_out_grad)


def solution(mesh):
    placed = (P("col", "row"), P("col", "row"), P("row", "col"), P("col", "row"))
    return jax.shard_map(
        on_device,
        mesh=mesh,
        in_specs=placed,
        out_specs=(P("col", "row"), P("row", "col"), P("col", "row")),
        check_vma=False,
    )
```

profile of v0, /device:TPU:1, one launch (start us, length us, event | category | flops | bytes accessed | tf_op | source)
XLA Modules:
  0.0 303.6 jit_solution(9570776879998448367)
XLA Ops:
  7.2 0.0 copy-start
  7.2 0.0 all-reduce.3.cloned.1.call-start
  7.2 49.1 %all_gather.7 = bf16[256,1792]{1,0:T(8,128)(2,1)S(1)} all-gather(bf16[8,1792]{1,0:T(8,128)(2,1)} %param.4), channel_id=1, replica_groups=mesh['row'=8,'col'=32] {'col'}, dimensions={0}, use_global_device_ids=true | all-gather | bytes 946176 | tf_op jit(solution)/shard_map/all_gather | solution.py:19
  56.3 0.0 copy-start.2
  56.3 39.4 %all_gather.6 = bf16[256,1792]{1,0:T(8,128)(2,1)S(1)} all-gather(bf16[8,1792]{1,0:T(8,128)(2,1)} %param.5), channel_id=1, replica_groups=mesh['row'=8,'col'=32] {'col'}, dimensions={0}, use_global_device_ids=true | all-gather | bytes 946176 | tf_op jit(solution)/shard_map/all_gather | solution.py:20
  95.7 0.9 copy-done.4
  96.7 3.9 %fusion.9 = f32[256,928]{0,1:T(8,128)} fusion(bf16[256,1792]{1,0:T(8,128)(2,1)S(1)} %all_gather.6, bf16[928,1792]{1,0:T(8,128)(2,1)} %param.7), kind=kOutput, calls=%fused_computation.13 | convolution fusion | flops 851443712 | bytes 5193728 | tf_op jit(solution)/shard_map/dot_general | solution.py:23
  100.6 0.0 copy-done.2
  100.6 0.0 copy-done
  100.6 2.0 fusion.10
  102.6 0.0 all-reduce.3.cloned.1.call-update
  102.6 0.0 reduce-scatter.2.cloned.1.call-start
  102.7 77.4 %all-reduce.3.cloned.1.call-done = (f32[256,928]{0,1:T(8,128)}, f32[256,928]{0,1:T(8,128)}) async-done(((f32[256,928]{0,1:T(8,128)}, f32[256,928]{0,1:T(8,128)}), (f32[256,928]{0,1:T(8,128)}, f32[256,928]{0,1:T(8,128)})) %all-reduce.3.cloned.1.call-update) | async-done | bytes 1900560 | tf_op jit(solution)/shard_map/psum | solution.py:26
  180.1 3.7 %convolution_convert_fusion.2 = bf16[256,1792]{1,0:T(8,128)(2,1)} fusion(bf16[1792,928]{0,1:T(8,128)(2,1)S(1)} %copy-done, f32[256,928]{0,1:T(8,128)} %get-tuple-element.3, f32[256,928]{0,1:T(8,128)} %get-tuple-element.4), kind=kOutput, calls=%fused_computation.3 | convolution fusion | flops 854278144 | bytes 6144000 | tf_op jit(solution)/shard_map/dot_general | solution.py:35
  183.7 0.0 reduce-scatter.2.cloned.1.call-update
  183.7 0.0 copy-start.1
  183.7 0.0 copy-start.3
  183.8 0.0 copy-start.5
  183.8 4.4 %convolution_convert_fusion = bf16[928,1792]{1,0:T(8,128)(2,1)} fusion(bf16[256,1792]{1,0:T(8,128)(2,1)} %copy-done.4, f32[256,928]{0,1:T(8,128)} %get-tuple-element.4), kind=kOutput, calls=%fused_computation | convolution fusion | flops 854294528 | bytes 5193728 | tf_op jit(solution)/shard_map/dot_general | solution.py:28
  188.2 0.0 copy-done.1
  188.2 0.0 copy-done.3
  188.2 0.0 copy-done.5
  188.2 3.0 fusion
  191.2 105.6 %reduce-scatter.2.cloned.1.call-done = bf16[8,1792]{1,0:T(8,128)(2,1)} async-done(((bf16[256,1792]{1,0:T(8,128)(2,1)}), bf16[8,1792]{1,0:T(8,128)(2,1)}) %reduce-scatter.2.cloned.1.call-update) | async-done | bytes 28688 | tf_op jit(solution)/shard_map/reduce_scatter | solution.py:34
  (1 shorter events, 0.0 us)
Async XLA Ops:
  7.2 93.4 %copy-start = (bf16[1792,928]{0,1:T(8,128)(2,1)S(1)}, bf16[1792,928]{0,1:T(8,128)(2,1)}, u32[]{:S(2)}) copy-start(bf16[1792,928]{0,1:T(8,128)(2,1)} %param.6) | copy-start | bytes 9977860
  7.2 172.9 %all-reduce.3.cloned.1.call-start = ((), (), s32[]{:S(2)}) async-start(), calls=%async_computation.2 | async-start | bytes 3801088 | tf_op jit(solution)/shard_map/psum | solution.py:26
  56.3 44.3 %copy-start.2 = (bf16[256,1792]{1,0:T(8,128)(2,1)}, bf16[256,1792]{1,0:T(8,128)(2,1)S(1)}, u32[]{:S(2)}) copy-start(bf16[256,1792]{1,0:T(8,128)(2,1)S(1)} %all_gather.7) | copy-start | bytes 2752516
  95.7 0.9 copy-start.4
  102.6 194.1 %reduce-scatter.2.cloned.1.call-start = ((), (), s32[]{:S(2)}) async-start(), calls=%async_computation.1 | async-start | bytes 946176 | tf_op jit(solution)/shard_map/reduce_scatter | solution.py:34
  183.7 4.5 %copy-start.1 = (f32[256,928]{0,1:T(8,128)S(1)}, f32[256,928]{0,1:T(8,128)}, u32[]{:S(2)}) copy-start(f32[256,928]{0,1:T(8,128)} %get-tuple-element.4) | copy-start | bytes 2850820
  183.7 4.4 %copy-start.3 = (bf16[256,1792]{1,0:T(8,128)(2,1)S(1)}, bf16[256,1792]{1,0:T(8,128)(2,1)}, u32[]{:S(2)}) copy-start(bf16[256,1792]{1,0:T(8,128)(2,1)} %copy-done.2) | copy-start | bytes 2752516
  183.8 4.4 %copy-start.5 = (f32[256,928]{0,1:T(8,128)S(1)}, f32[256,928]{0,1:T(8,128)}, u32[]{:S(2)}) copy-start(f32[256,928]{0,1:T(8,128)} %get-tuple-element.3) | copy-start | bytes 2850820
Sparse Core Ops, SparseCore 0:
  102.7 77.2 all-reduce.2
  185.2 111.5 reduce-scatter.1
where the time goes:
time: 308 us; the launch traced here: 304 us
  waiting for transfers between devices  183 us (59%)
  blocking collectives  88.5 us (29%)
  matrix products  17 us (6%)
  between operations  14.1 us (5%)
    reduce_scatter x1, waiting for transfers between devices, on_device(): lax.psum_scatter(lax.dot_general(pre_grad, w_in, (((1,), (1,)), ((), ()))...  106 us
    psum x1, waiting for transfers between devices, on_device(): pre, back = lax.psum((pre_part, back_part), 'row')  77.4 us
    all_gather x1, blocking collectives, on_device(): lax.all_gather(inputs, 'col', axis=0, tiled=True)  49.1 us
    all_gather x1, blocking collectives, on_device(): lax.all_gather(out_grad, 'col', axis=0, tiled=True)  39.4 us
  transfers between devices with their start and end apart: 2, of which 2 were waited for; matrix products, arithmetic and copies ran while one was open for 2% of the time, Pallas kernels for 0%

commit v1 on v0

v1 whole, which is shorter than its diff:
```python
import functools
import math

import jax
import jax.numpy as jnp
from jax import lax
from jax.experimental import pallas as pl
from jax.experimental.pallas import tpu as pltpu
from jax.sharding import PartitionSpec as P

MESH = pl.DeviceIdType.MESH
BF16, F32 = jnp.bfloat16, jnp.float32
NT = (((1,), (1,)), ((), ()))
NN = (((1,), (0,)), ((), ()))
TN = (((0,), (0,)), ((), ()))

T = 8
D = 1792
HALF = D // 2
F = 928
ROWS = 8

BLOCKS = (
    (0, 0), (0, 1), (0, -1), (1, 0),
    (0, 2), (0, -2), (1, 1), (1, -1),
    (0, 3), (0, -3), (1, 2), (1, -2),
    (0, 4), (1, 3), (1, -3), (1, 4),
)
SLOT = {block: i for i, block in enumerate(BLOCKS)}
BATCHES = 4
PER = len(BLOCKS) // BATCHES
TB = PER * 2 * T


def dot(a, b, dims):
    return lax.dot_general(a, b, dims, preferred_element_type=F32)


def mirrored(block):
    y, d = block
    return SLOT[(y, d if d == 4 else -d)]


def stack(a, b):
    return jnp.concatenate([a, b], axis=0)


def fetch_wait(ref, sem):
    pltpu.make_async_copy(ref, ref, sem).wait()


def kernel(
    x_in_hbm, x_og_hbm, w_in_hbm, w_out_hbm,
    in_grad, w_in_grad, w_out_grad,
    x, w_in, w_out, mine, sibs, acts, part, part_in, act, hid, pgr, to_sib, keep, from_sib, comb, comb_in,
    x_sem, w_sem, mine_sem, sibs_sem, part_sem, act_sem, fs_sem, comb_sem,
    mine_out, sibs_out, part_out, act_out, fs_out, comb_out,
):
    r, c = lax.axis_index("row"), lax.axis_index("col")
    y_hi, z, k = c // 16, lax.rem(c // 2, 8), lax.rem(c, 2)

    def chip(y, d):
        return (r, lax.rem(y_hi + y, 2) * 16 + lax.rem(z + d + 8, 8) * 2 + k)

    sibling = (r, c + 1 - 2 * k)

    def peer(j):
        return lax.rem(r + j, ROWS)

    def send(src, dst, out, sem, to):
        pltpu.make_async_remote_copy(
            src_ref=src, dst_ref=dst, send_sem=out, recv_sem=sem, device_id=to, device_id_type=MESH
        ).start()

    weights = [pltpu.make_async_copy(w_in_hbm, w_in, w_sem.at[0]), pltpu.make_async_copy(w_out_hbm, w_out, w_sem.at[1])]
    tokens = [pltpu.make_async_copy(x_in_hbm, x.at[0], x_sem.at[0]), pltpu.make_async_copy(x_og_hbm, x.at[1], x_sem.at[1])]
    for copy in tokens + weights:
        copy.start()

    barrier = pltpu.get_barrier_semaphore()
    friends = [chip(*block) for block in BLOCKS[1:]] + [sibling] + [(peer(j), c) for j in range(1, ROWS)]
    for friend in friends:
        pl.semaphore_signal(barrier, inc=1, device_id=friend, device_id_type=MESH)
    for a in range(2):
        tokens[a].wait()
        block = x[a].astype(F32)
        mine[0, a] = stack(block[:, :HALF], block[:, HALF:]).astype(BF16)
    pl.semaphore_wait(barrier, len(friends))

    def hop(block, onward, to):
        slot = SLOT[onward]
        send(mine.at[SLOT[block]], mine.at[slot], mine_out, mine_sem.at[slot], to)

    def share(block):
        slot = SLOT[block]
        send(mine.at[slot], sibs.at[slot], sibs_out, sibs_sem.at[slot // PER], sibling)

    def forward(block):
        y, d = block
        if block == (0, 0):
            hop(block, (1, 0), chip(1, 0))
        if 0 <= d < 3 or block == (0, 3):
            hop(block, (y, d + 1), chip(0, -1))
        if -3 < d <= 0 or block == (1, -3):
            hop(block, (y, 4 if d == -3 else d - 1), chip(0, 1))
        share(block)

    def arrive(block):
        slot = SLOT[block]
        fetch_wait(mine.at[slot], mine_sem.at[slot])
        forward(block)

    def up(b):
        fetch_wait(sibs.at[pl.ds(PER * b, PER)], sibs_sem.at[b])
        for s in range(PER * b, PER * b + PER):
            for a in range(2):
                own, sib = mine[s, a], sibs[s, a]
                acts[a, 16 * s : 16 * s + 16, :HALF] = stack(own[:T], sib[:T])
                acts[a, 16 * s : 16 * s + 16, HALF:] = stack(own[T:], sib[T:])
        rows = slice(TB * b, TB * b + TB)
        pre = dot(acts[0, rows], w_in[...], NT)
        back = dot(acts[1, rows], w_out[...], NT)
        for i in range(ROWS):
            part[b, i] = stack(pre[T * i : T * i + T], back[T * i : T * i + T]).astype(BF16)
        for j in range(1, ROWS):
            send(part.at[b, peer(j)], part_in.at[b, j - 1], part_out.at[b], part_sem.at[b], (peer(j), c))

    def activate(b):
        fetch_wait(part_in.at[b], part_sem.at[b])
        total = part[b, r].astype(F32)
        for j in range(ROWS - 1):
            total += part_in[b, j].astype(F32)
        pre, back = total[:T], total[T:]
        cdf = 0.5 * (1.0 + lax.erf(pre * (1.0 / math.sqrt(2.0))))
        slope = cdf + pre * jnp.exp(-0.5 * pre * pre) * (1.0 / math.sqrt(2.0 * math.pi))
        act[b, r] = stack(pre * cdf, back * slope).astype(BF16)
        for j in range(1, ROWS):
            send(act.at[b, r], act.at[b, r], act_out.at[b], act_sem.at[b], (peer(j), c))

    def down(b):
        fetch_wait(act.at[b, pl.ds(0, ROWS - 1)], act_sem.at[b])
        for i in range(0, ROWS, 2):
            one, two = act[b, i], act[b, i + 1]
            at = TB * b + T * i
            hid[at : at + 16] = stack(one[:T], two[:T])
            pgr[at : at + 16] = stack(one[T:], two[T:])
        grad = dot(pgr[TB * b : TB * b + TB], w_in[...], NN)
        for i in range(PER):
            own, sib = grad[16 * i : 16 * i + T], grad[16 * i + T : 16 * i + 16]
            to_sib[b, i] = stack(sib[:, :HALF], sib[:, HALF:]).astype(BF16)
            keep[b, i] = stack(own[:, :HALF], own[:, HALF:])
        send(to_sib.at[b], from_sib.at[b], fs_out.at[b], fs_sem.at[b], sibling)

    def combine(b):
        fetch_wait(from_sib.at[b], fs_sem.at[b])
        for i in range(PER):
            s = PER * b + i
            total = keep[b, i] + from_sib[b, i].astype(F32)
            if s == 0:
                keep[0, 0] = total
            else:
                comb[s] = total.astype(BF16)
                send(comb.at[s], comb_in.at[mirrored(BLOCKS[s])], comb_out.at[b], comb_sem.at[b], chip(*BLOCKS[s]))

    forward((0, 0))
    for block in ((0, 1), (0, -1), (1, 0)):
        arrive(block)
    for copy in weights:
        copy.wait()
    for block in ((0, 2), (0, -2), (1, 1), (1, -1)):
        arrive(block)
    up(0)
    for block in ((0, 3), (0, -3), (1, 2), (1, -2)):
        arrive(block)
    up(1)
    activate(0)
    for block in ((0, 4), (1, 3), (1, -3)):
        arrive(block)
    up(2)
    activate(1)
    arrive((1, 4))
    down(0)
    up(3)
    activate(2)
    down(1)
    combine(0)
    activate(3)
    down(2)
    combine(1)
    down(3)
    combine(2)
    combine(3)
    w_out_grad[...] = dot(hid[...], acts[1], TN).astype(BF16)
    w_in_grad[...] = dot(pgr[...], acts[0], TN).astype(BF16)
    total = keep[0, 0]
    for b in range(BATCHES):
        low = max(PER * b, 1)
        fetch_wait(comb_in.at[pl.ds(low, PER * (b + 1) - low)], comb_sem.at[b])
        for s in range(low, PER * (b + 1)):
            total += comb_in[s].astype(F32)
    in_grad[:, :HALF] = total[:T].astype(BF16)
    in_grad[:, HALF:] = total[T:].astype(BF16)

    fetch_wait(mine.at[pl.ds(1, len(BLOCKS) - 1)], mine_out)
    fetch_wait(sibs, sibs_out)
    for b in range(BATCHES):
        low = max(PER * b, 1)
        fetch_wait(part_in.at[b], part_out.at[b])
        fetch_wait(act.at[b, pl.ds(0, ROWS - 1)], act_out.at[b])
        fetch_wait(to_sib.at[b], fs_out.at[b])
        fetch_wait(comb.at[pl.ds(low, PER * (b + 1) - low)], comb_out.at[b])


PIECES = 2


def flush(x, gi, go, x_hbm, gi_hbm, go_hbm, sem):
    copies = [pltpu.make_async_copy(x, x_hbm, sem.at[2 * PIECES])]
    n = F // PIECES
    for i in range(PIECES):
        at = pl.ds(n * i, n)
        copies.append(pltpu.make_async_copy(gi.at[at], gi_hbm.at[at], sem.at[2 * i]))
        copies.append(pltpu.make_async_copy(go.at[at], go_hbm.at[at], sem.at[2 * i + 1]))
    for copy in copies:
        copy.start()
    for copy in copies:
        copy.wait()


def on_device(inputs, out_grad, w_in, w_out):
    vmem = pl.BlockSpec(memory_space=pltpu.VMEM)
    hbm = pl.BlockSpec(memory_space=pl.ANY)
    n = len(BLOCKS)
    dma = pltpu.SemaphoreType.DMA
    outs = pl.pallas_call(
        kernel,
        out_shape=(pltpu.VMEM((T, D), BF16), pltpu.VMEM((F, D), BF16), pltpu.VMEM((F, D), BF16)),
        in_specs=[hbm] * 4,
        out_specs=(vmem, vmem, vmem),
        scratch_shapes=[
            pltpu.VMEM((2, T, D), BF16),
            pltpu.VMEM((F, D), BF16),
            pltpu.VMEM((F, D), BF16),
            pltpu.VMEM((n, 2, 16, HALF), BF16),
            pltpu.VMEM((n, 2, 16, HALF), BF16),
            pltpu.VMEM((2, 16 * n, D), BF16),
            pltpu.VMEM((BATCHES, ROWS, 16, F), BF16),
            pltpu.VMEM((BATCHES, ROWS - 1, 16, F), BF16),
            pltpu.VMEM((BATCHES, ROWS, 16, F), BF16),
            pltpu.VMEM((16 * n, F), BF16),
            pltpu.VMEM((16 * n, F), BF16),
            pltpu.VMEM((BATCHES, PER, 16, HALF), BF16),
            pltpu.VMEM((BATCHES, PER, 16, HALF), F32),
            pltpu.VMEM((BATCHES, PER, 16, HALF), BF16),
            pltpu.VMEM((n, 16, HALF), BF16),
            pltpu.VMEM((n, 16, HALF), BF16),
            dma((2,)),
            dma((2,)),
            dma((n,)),
            dma((BATCHES,)),
            dma((BATCHES,)),
            dma((BATCHES,)),
            dma((BATCHES,)),
            dma((BATCHES,)),
            dma,
            dma,
            dma((BATCHES,)),
            dma((BATCHES,)),
            dma((BATCHES,)),
            dma((BATCHES,)),
        ],
        compiler_params=pltpu.CompilerParams(collective_id=0, has_side_effects=True, vmem_limit_bytes=44 << 20),
        name="block",
    )(*(pltpu.with_memory_space_constraint(a, pltpu.HBM) for a in (inputs, out_grad, w_in.T, w_out)))
    in_grad, w_in_grad, w_out_grad = pl.pallas_call(
        flush,
        out_shape=tuple(jax.ShapeDtypeStruct(o.shape, BF16) for o in outs),
        in_specs=[vmem] * 3,
        out_specs=(hbm,) * 3,
        scratch_shapes=[dma((2 * PIECES + 1,))],
        compiler_params=pltpu.CompilerParams(vmem_limit_bytes=16 << 20),
        name="flush",
    )(*outs)
    return (in_grad, w_in_grad.T, w_out_grad)


def solution(mesh):
    placed = (P("col", "row"), P("col", "row"), P("row", "col"), P("col", "row"))
    return jax.shard_map(
        on_device,
        mesh=mesh,
        in_specs=placed,
        out_specs=(P("col", "row"), P("row", "col"), P("col", "row")),
        check_vma=False,
    )
```

time: 308 us -> 63.9 us (0.21); the launches traced: 304 us -> 63.8 us
  waiting for transfers between devices: 183 us -> 0 us
  blocking collectives: 88.5 us -> 0 us
  Pallas kernels: 0 us -> 63.2 us
  matrix products: 17 us -> 0 us
  between operations: 14.1 us -> 0.64 us
    reduce_scatter x1 -> x0, waiting for transfers between devices: 106 us -> none  [on_device(): lax.psum_scatter(lax.dot_general(pre_grad, w_in, (((1,), (1,)), ((), ()))...]
    all_gather x2 -> x0, blocking collectives: 88.5 us -> none  [the longest x1 49.1 us: on_device(): lax.all_gather(inputs, 'col', axis=0, tiled=True)]
    psum x1 -> x0, waiting for transfers between devices: 77.4 us -> none  [on_device(): pre, back = lax.psum((pre_part, back_part), 'row')]
    pallas_call x0 -> x2, Pallas kernels: none -> 63.2 us  [the longest x1 60.3 us: on_device(): pl.pallas_call(kernel, out_shape=(pltpu.VMEM((T, D), BF16), pltpu.VMEM((F...]
    dot_general x5 -> x0, matrix products: 17 us -> none  [the longest x1 4.42 us: on_device(): lax.dot_general(hidden, full_grad, (((0,), (0,)), ((), ())), preferred_el...]
  transfers between devices with their start and end apart: 2 -> 0, of which waited for: 2 -> 0; matrix products, arithmetic and copies ran while one was open for 2% -> 0% of each run, Pallas kernels for 0% -> 0%
where the time goes in v1:
time: 63.9 us; the launch traced here: 63.8 us
  Pallas kernels  63.2 us (99%)
  between operations  0.64 us (1%)
    pallas_call x1, Pallas kernels, on_device(): pl.pallas_call(kernel, out_shape=(pltpu.VMEM((T, D), BF16), pltpu.VMEM((F...  60.3 us
    pallas_call x1, Pallas kernels, on_device(): pl.pallas_call(flush, out_shape=tuple((jax.ShapeDtypeStruct(o.shape, BF16...  2.87 us

profile of v1, /device:TPU:1, one launch (start us, length us, event | category | flops | bytes accessed | tf_op | source)
XLA Modules:
  0.0 63.8 jit_solution(1811124476571152360)
XLA Ops:
  0.6 60.3 %block.1 = (bf16[8,1792]{1,0:T(8,128)(2,1)S(1)}, bf16[928,1792]{1,0:T(8,128)(2,1)S(1)}, bf16[928,1792]{1,0:T(8,128)(2,1)S(1)}) custom-call(bf16[8,1792]{1,0:T(8,128)(2,1)} %x_in_hbm.1, bf16[8,1792]{1,0:T(8,128)(2,1)} %x_og_hbm.1, bf16[928,1792]{1,0:T(8,128)(2,1)} %bitcast.2, bf16[928,1792]{1,0:T(8,128)(2,1)} %w_out_hbm.1), custom_call_target="tpu_custom_call" | custom-call | tf_op jit(solution)/shard_map/block/pallas_call | solution.py:235
  61.0 2.9 %flush.1 = (bf16[8,1792]{1,0:T(8,128)(2,1)}, bf16[928,1792]{1,0:T(8,128)(2,1)}, bf16[928,1792]{1,0:T(8,128)(2,1)}) custom-call(bf16[8,1792]{1,0:T(8,128)(2,1)S(1)} %get-tuple-element.9.x, bf16[928,1792]{1,0:T(8,128)(2,1)S(1)} %get-tuple-element.10.gi, bf16[928,1792]{1,0:T(8,128)(2,1)S(1)} %get-tuple-element.11.go), custom_call_target="tpu_custom_call" | custom-call | tf_op jit(solution)/shard_map/flush/pallas_call | solution.py:275

commit v2 on v1

v2 whole, which is shorter than its diff:
```python
import functools
import math

import jax
import jax.numpy as jnp
from jax import lax
from jax.experimental import pallas as pl
from jax.experimental.pallas import tpu as pltpu
from jax.sharding import PartitionSpec as P

MESH = pl.DeviceIdType.MESH
BF16, F32 = jnp.bfloat16, jnp.float32
NT = (((1,), (1,)), ((), ()))
NN = (((1,), (0,)), ((), ()))
TN = (((0,), (0,)), ((), ()))

T = 8
D = 1792
HALF = D // 2
F = 928
WIDE = 512
ROWS = 8

BLOCKS = (
    (0, 1), (0, -1), (1, 0), (0, 2),
    (0, -2), (1, 1), (1, -1), (0, 3),
    (0, -3), (1, 2), (1, -2), (0, 4),
    (1, 3), (1, -3), (1, 4), (0, 0),
)
ONWARD = {
    (0, 0): ((0, 2), (0, -2), (1, 0), (0, 1), (0, -1)),
    (0, 1): ((1, 0),),
    (0, -1): ((1, 0),),
    (0, 2): ((0, -1), (1, 0)),
    (0, -2): ((0, 1), (1, 0)),
    (0, 4): ((1, 0),),
    (1, 2): ((0, -1),),
    (1, -2): ((0, 1),),
}
SLOT = {block: i for i, block in enumerate(BLOCKS)}
HOME = SLOT[(0, 0)]
BATCHES = 4
PER = len(BLOCKS) // BATCHES
TB = PER * 2 * T


SUM_DIRECT = (2, 3)
SPREAD_DIRECT = (0, 1, 2, 3)


def dot(a, b, dims):
    return lax.dot_general(a, b, dims, preferred_element_type=F32)


def mirrored(block):
    y, d = block
    return SLOT[(y, d if d == 4 else -d)]


def stack(a, b):
    return jnp.concatenate([a, b], axis=0)


def folded(x):
    pad = jnp.zeros((T, 2 * WIDE - F), F32)
    return stack(x[:, :WIDE], jnp.concatenate([x[:, WIDE:], pad], axis=1)).astype(BF16)


def unfold(ref, at, one, two):
    ref[at : at + 16, :WIDE] = stack(one[:T], two[:T])
    ref[at : at + 16, WIDE:] = stack(one[T:, : F - WIDE], two[T:, : F - WIDE])


def fetch_wait(ref, sem):
    pltpu.make_async_copy(ref, ref, sem).wait()


def kernel(
    x_in_hbm, x_og_hbm, w_in_hbm, w_out_hbm,
    in_grad, w_in_grad, w_out_grad,
    x, w_in, w_out, w_in_t, w_out_t, mine, sibs, acts, part, part_in, x_in, y_to, y_in, own_row, act, late, hid, pgr, to_sib, keep, from_sib, comb, comb_in,
    x_sem, w_sem, mine_sem, sibs_sem, part_sem, y_sem, act_sem, act_y_sem, late_sem, late_y_sem, fs_sem, comb_sem,
    mine_out, sibs_out, part_out, y_out, act_out, late_out, fs_out, comb_out,
):
    r, c = lax.axis_index("row"), lax.axis_index("col")
    y_hi, z, k = c // 16, lax.rem(c // 2, 8), lax.rem(c, 2)

    def chip(y, d):
        return (r, lax.rem(y_hi + y, 2) * 16 + lax.rem(z + d + 8, 8) * 2 + k)

    sibling = (r, c + 1 - 2 * k)

    y_lo, x_at = r // 4, lax.rem(r, 4)
    me = 2 * x_at + y_lo
    y_peer = (lax.rem(r + 4, ROWS), c)

    def peer(j):
        return lax.rem(r + j, ROWS)

    def x_peer(j):
        return (4 * y_lo + lax.rem(x_at + j, 4), c)

    def send(src, dst, out, sem, to):
        pltpu.make_async_remote_copy(
            src_ref=src, dst_ref=dst, send_sem=out, recv_sem=sem, device_id=to, device_id_type=MESH
        ).start()

    weights = [pltpu.make_async_copy(w_in_hbm, w_in, w_sem.at[0]), pltpu.make_async_copy(w_out_hbm, w_out, w_sem.at[1])]
    tokens = [pltpu.make_async_copy(x_in_hbm, x.at[0], x_sem.at[0]), pltpu.make_async_copy(x_og_hbm, x.at[1], x_sem.at[1])]
    for copy in tokens + weights:
        copy.start()

    barrier = pltpu.get_barrier_semaphore()
    friends = [chip(*block) for block in ONWARD[(0, 0)]] + [sibling] + [(peer(j), c) for j in range(1, ROWS)]
    for friend in friends:
        pl.semaphore_signal(barrier, inc=1, device_id=friend, device_id_type=MESH)
    for a in range(2):
        tokens[a].wait()
        block = x[a].astype(F32)
        mine[HOME, a] = stack(block[:, :HALF], block[:, HALF:]).astype(BF16)
    pl.semaphore_wait(barrier, len(friends))

    def forward(block):
        slot = SLOT[block]
        for to in ONWARD.get(block, ()):
            seen = SLOT[((block[0] + to[0]) % 2, block[1] - to[1])]
            send(mine.at[slot], mine.at[seen], mine_out, mine_sem.at[seen], chip(*to))
        if block == (0, -2):
            far, near = SLOT[(0, 4)], SLOT[(0, 2)]
            send(mine.at[near + k * (slot - near)], mine.at[far], mine_out, mine_sem.at[far], chip(0, 4 * k - 2))
        send(mine.at[slot], sibs.at[slot], sibs_out, sibs_sem.at[slot], sibling)

    def arrive(*blocks):
        for block in blocks:
            slot = SLOT[block]
            fetch_wait(mine.at[slot], mine_sem.at[slot])
            forward(block)

    sums = {}

    def up_in(b):
        for s in range(PER * b, PER * b + PER):
            fetch_wait(sibs.at[s], sibs_sem.at[s])
            for a in range(2):
                own, sib = mine[s, a], sibs[s, a]
                acts[a, 16 * s : 16 * s + 16, :HALF] = stack(own[:T], sib[:T])
                acts[a, 16 * s : 16 * s + 16, HALF:] = stack(own[T:], sib[T:])
        sums[b] = dot(acts[0, TB * b : TB * b + TB], w_in_t[...], NN)

    def up_og(b):
        pre, back = sums[b], dot(acts[1, TB * b : TB * b + TB], w_out_t[...], NN)
        for i in range(ROWS):
            part[b, i // 2, i % 2] = stack(pre[T * i : T * i + T], back[T * i : T * i + T]).astype(BF16)
        if b in SUM_DIRECT:
            for j in range(1, ROWS):
                to = peer(j)
                send(part.at[b, lax.rem(to, 4), to // 4], part_in.at[b, j - 1], part_out.at[b], part_sem.at[b], (to, c))
        else:
            for j in range(1, 4):
                send(part.at[b, lax.rem(x_at + j, 4)], x_in.at[b, j - 1], part_out.at[b], part_sem.at[b], x_peer(j))

    def along_x(b):
        if b in SUM_DIRECT:
            return
        fetch_wait(x_in.at[b], part_sem.at[b])

        def over_x(lane):
            total = part[b, x_at, lane].astype(F32)
            for j in range(3):
                total += x_in[b, j, lane].astype(F32)
            return total

        y_to[b] = over_x(1 - y_lo).astype(BF16)
        send(y_to.at[b], y_in.at[b], y_out.at[b], y_sem.at[b], y_peer)
        own_row[b] = over_x(y_lo)

    def activate(b):
        if b in SUM_DIRECT:
            fetch_wait(part_in.at[b], part_sem.at[b])
            total = part[b, x_at, y_lo].astype(F32)
            for j in range(ROWS - 1):
                total += part_in[b, j].astype(F32)
        else:
            fetch_wait(y_in.at[b], y_sem.at[b])
            total = own_row[b] + y_in[b].astype(F32)
        pre, back = total[:T], total[T:]
        cdf = 0.5 * (1.0 + lax.erf(pre * (1.0 / math.sqrt(2.0))))
        slope = cdf + pre * jnp.exp(-0.5 * pre * pre) * (1.0 / math.sqrt(2.0 * math.pi))
        act[b, me] = folded(back * slope)
        late[me, b] = folded(pre * cdf)
        own = act.at[b, me]
        if b in SPREAD_DIRECT:
            for j in range(1, ROWS):
                send(own, own, act_out.at[b], act_sem.at[b], (peer(j), c))
        else:
            send(own, own, act_out.at[b], act_y_sem.at[b], y_peer)
            for j in range(1, 4):
                send(own, own, act_out.at[b], act_sem.at[b], x_peer(j))

    def relay(b):
        if b in SPREAD_DIRECT:
            return
        other = act.at[b, 2 * x_at + 1 - y_lo]
        fetch_wait(other, act_y_sem.at[b])
        for j in range(1, 4):
            send(other, other, act_out.at[b], act_sem.at[b], x_peer(j))

    def spread_late():
        own = late.at[me]
        send(own, own, late_out, late_y_sem, y_peer)
        for j in range(1, 4):
            send(own, own, late_out, late_sem, x_peer(j))

    def relay_late():
        other = late.at[2 * x_at + 1 - y_lo]
        fetch_wait(other, late_y_sem)
        for j in range(1, 4):
            send(other, other, late_out, late_sem, x_peer(j))

    def down(b):
        fetch_wait(act.at[b, pl.ds(0, ROWS - (1 if b in SPREAD_DIRECT else 2))], act_sem.at[b])
        for i in range(0, ROWS, 2):
            unfold(pgr, TB * b + T * i, act[b, i], act[b, i + 1])
        grad = dot(pgr[TB * b : TB * b + TB], w_in[...], NN)
        for i in range(PER):
            own, sib = grad[16 * i : 16 * i + T], grad[16 * i + T : 16 * i + 16]
            to_sib[b, i] = stack(sib[:, :HALF], sib[:, HALF:]).astype(BF16)
            keep[b, i] = stack(own[:, :HALF], own[:, HALF:])
        send(to_sib.at[b], from_sib.at[b], fs_out.at[b], fs_sem.at[b], sibling)

    def combine(b):
        fetch_wait(from_sib.at[b], fs_sem.at[b])
        for i in range(PER):
            s = PER * b + i
            total = keep[b, i] + from_sib[b, i].astype(F32)
            if s == HOME:
                keep[b, i] = total
            else:
                comb[s] = total.astype(BF16)
                seen = mirrored(BLOCKS[s])
                send(comb.at[s], comb_in.at[seen], comb_out, comb_sem.at[seen], chip(*BLOCKS[s]))

    forward((0, 0))
    weights[0].wait()
    w_in_t[...] = w_in[...].T
    weights[1].wait()
    w_out_t[...] = w_out[...].T
    arrive((0, 2), (0, -2), (0, 1), (0, -1), (1, 0))
    up_in(0)
    up_og(0)
    arrive((1, 2), (1, -2), (0, 4), (1, 1), (1, -1), (0, 3), (0, -3))
    up_in(1)
    up_og(1)
    along_x(0)
    up_in(2)
    arrive((1, 3), (1, -3))
    up_og(2)
    activate(0)
    arrive((1, 4))
    up_in(3)
    along_x(1)
    up_og(3)
    activate(1)
    along_x(2)
    activate(2)
    down(0)
    combine(0)
    along_x(3)
    activate(3)
    spread_late()
    down(1)
    combine(1)
    down(2)
    combine(2)
    relay_late()
    down(3)
    combine(3)
    w_in_grad[...] = dot(pgr[...], acts[0], TN).astype(BF16)
    fetch_wait(late.at[pl.ds(0, ROWS - 2)], late_sem)
    for b in range(BATCHES):
        for i in range(0, ROWS, 2):
            unfold(hid, TB * b + T * i, late[i, b], late[i + 1, b])
    w_out_grad[...] = dot(hid[...], acts[1], TN).astype(BF16)
    total = keep[HOME // PER, HOME % PER]
    for s in range(len(BLOCKS)):
        if s == HOME:
            continue
        fetch_wait(comb_in.at[s], comb_sem.at[s])
        total += comb_in[s].astype(F32)
    in_grad[:, :HALF] = total[:T].astype(BF16)
    in_grad[:, HALF:] = total[T:].astype(BF16)

    fetch_wait(mine.at[pl.ds(0, len(BLOCKS) - 1)], mine_out)
    fetch_wait(sibs, sibs_out)
    fetch_wait(late.at[pl.ds(0, ROWS - 1)], late_out)
    fetch_wait(comb.at[pl.ds(0, len(BLOCKS) - 1)], comb_out)
    for b in range(BATCHES):
        if b in SUM_DIRECT:
            fetch_wait(part_in.at[b], part_out.at[b])
        else:
            fetch_wait(x_in.at[b], part_out.at[b])
            fetch_wait(y_in.at[b], y_out.at[b])
        fetch_wait(act.at[b, pl.ds(0, ROWS - 1)], act_out.at[b])
        fetch_wait(to_sib.at[b], fs_out.at[b])


PIECES = 2


def flush(x, gi, go, x_hbm, gi_hbm, go_hbm, sem):
    copies = [pltpu.make_async_copy(x, x_hbm, sem.at[2 * PIECES])]
    n = F // PIECES
    for i in range(PIECES):
        at = pl.ds(n * i, n)
        copies.append(pltpu.make_async_copy(gi.at[at], gi_hbm.at[at], sem.at[2 * i]))
        copies.append(pltpu.make_async_copy(go.at[at], go_hbm.at[at], sem.at[2 * i + 1]))
    for copy in copies:
        copy.start()
    for copy in copies:
        copy.wait()


def on_device(inputs, out_grad, w_in, w_out):
    vmem = pl.BlockSpec(memory_space=pltpu.VMEM)
    hbm = pl.BlockSpec(memory_space=pl.ANY)
    n = len(BLOCKS)
    dma = pltpu.SemaphoreType.DMA
    outs = pl.pallas_call(
        kernel,
        out_shape=(pltpu.VMEM((T, D), BF16), pltpu.VMEM((F, D), BF16), pltpu.VMEM((F, D), BF16)),
        in_specs=[hbm] * 4,
        out_specs=(vmem, vmem, vmem),
        scratch_shapes=[
            pltpu.VMEM((2, T, D), BF16),
            pltpu.VMEM((F, D), BF16),
            pltpu.VMEM((F, D), BF16),
            pltpu.VMEM((D, F), BF16),
            pltpu.VMEM((D, F), BF16),
            pltpu.VMEM((n, 2, 16, HALF), BF16),
            pltpu.VMEM((n, 2, 16, HALF), BF16),
            pltpu.VMEM((2, 16 * n, D), BF16),
            pltpu.VMEM((BATCHES, 4, 2, 16, F), BF16),
            pltpu.VMEM((BATCHES, ROWS - 1, 16, F), BF16),
            pltpu.VMEM((BATCHES, 3, 2, 16, F), BF16),
            pltpu.VMEM((BATCHES, 16, F), BF16),
            pltpu.VMEM((BATCHES, 16, F), BF16),
            pltpu.VMEM((BATCHES, 16, F), F32),
            pltpu.VMEM((BATCHES, ROWS, 16, WIDE), BF16),
            pltpu.VMEM((ROWS, BATCHES, 16, WIDE), BF16),
            pltpu.VMEM((16 * n, F), BF16),
            pltpu.VMEM((16 * n, F), BF16),
            pltpu.VMEM((BATCHES, PER, 16, HALF), BF16),
            pltpu.VMEM((BATCHES, PER, 16, HALF), F32),
            pltpu.VMEM((BATCHES, PER, 16, HALF), BF16),
            pltpu.VMEM((n, 16, HALF), BF16),
            pltpu.VMEM((n, 16, HALF), BF16),
            dma((2,)),
            dma((2,)),
            dma((n,)),
            dma((n,)),
            dma((BATCHES,)),
            dma((BATCHES,)),
            dma((BATCHES,)),
            dma((BATCHES,)),
            dma,
            dma,
            dma((BATCHES,)),
            dma((n,)),
            dma,
            dma,
            dma((BATCHES,)),
            dma((BATCHES,)),
            dma((BATCHES,)),
            dma,
            dma((BATCHES,)),
            dma,
        ],
        compiler_params=pltpu.CompilerParams(collective_id=0, has_side_effects=True, vmem_limit_bytes=44 << 20),
        name="block",
    )(*(pltpu.with_memory_space_constraint(a, pltpu.HBM) for a in (inputs, out_grad, w_in.T, w_out)))
    in_grad, w_in_grad, w_out_grad = pl.pallas_call(
        flush,
        out_shape=tuple(jax.ShapeDtypeStruct(o.shape, BF16) for o in outs),
        in_specs=[vmem] * 3,
        out_specs=(hbm,) * 3,
        scratch_shapes=[dma((2 * PIECES + 1,))],
        compiler_params=pltpu.CompilerParams(vmem_limit_bytes=16 << 20),
        name="flush",
    )(*outs)
    return (in_grad, w_in_grad.T, w_out_grad)


def solution(mesh):
    placed = (P("col", "row"), P("col", "row"), P("row", "col"), P("col", "row"))
    return jax.shard_map(
        on_device,
        mesh=mesh,
        in_specs=placed,
        out_specs=(P("col", "row"), P("row", "col"), P("col", "row")),
        check_vma=False,
    )
```

time: 63.9 us -> 56.1 us (0.88)
  Pallas kernels: 63.2 us -> 54.9 us
    pallas_call x1, Pallas kernels: 60.3 us -> 52.1 us  [on_device(): pl.pallas_call(kernel, out_shape=(pltpu.VMEM((T, D), BF16), pltpu.VMEM((F...]
where the time goes in v2:
time: 56.1 us; the launch traced here: 55.6 us
  Pallas kernels  54.9 us (98%)
  between operations  0.64 us (1%)
    pallas_call x1, Pallas kernels, on_device(): pl.pallas_call(kernel, out_shape=(pltpu.VMEM((T, D), BF16), pltpu.VMEM((F...  52.1 us
    pallas_call x1, Pallas kernels, on_device(): pl.pallas_call(flush, out_shape=tuple((jax.ShapeDtypeStruct(o.shape, BF16...  2.87 us

profile of v2, /device:TPU:1, one launch (start us, length us, event | category | flops | bytes accessed | tf_op | source)
XLA Modules:
  0.0 55.6 jit_solution(7675789336757394008)
XLA Ops:
  0.6 52.1 %block.1 = (bf16[8,1792]{1,0:T(8,128)(2,1)S(1)}, bf16[928,1792]{1,0:T(8,128)(2,1)S(1)}, bf16[928,1792]{1,0:T(8,128)(2,1)S(1)}) custom-call(bf16[8,1792]{1,0:T(8,128)(2,1)} %x_in_hbm.1, bf16[8,1792]{1,0:T(8,128)(2,1)} %x_og_hbm.1, bf16[928,1792]{1,0:T(8,128)(2,1)} %bitcast.2, bf16[928,1792]{1,0:T(8,128)(2,1)} %w_out_hbm.1), custom_call_target="tpu_custom_call" | custom-call | tf_op jit(solution)/shard_map/block/pallas_call | solution.py:328
  52.7 2.9 %flush.1 = (bf16[8,1792]{1,0:T(8,128)(2,1)}, bf16[928,1792]{1,0:T(8,128)(2,1)}, bf16[928,1792]{1,0:T(8,128)(2,1)}) custom-call(bf16[8,1792]{1,0:T(8,128)(2,1)S(1)} %get-tuple-element.9.x, bf16[928,1792]{1,0:T(8,128)(2,1)S(1)} %get-tuple-element.10.gi, bf16[928,1792]{1,0:T(8,128)(2,1)S(1)} %get-tuple-element.11.go), custom_call_target="tpu_custom_call" | custom-call | tf_op jit(solution)/shard_map/flush/pallas_call | solution.py:381

commit v3 on v2

v3 whole, which is shorter than its diff:
```python
import functools
import math

import jax
import jax.numpy as jnp
from jax import lax
from jax.experimental import pallas as pl
from jax.experimental.pallas import tpu as pltpu
from jax.sharding import PartitionSpec as P

MESH = pl.DeviceIdType.MESH
BF16, F32 = jnp.bfloat16, jnp.float32
NT = (((1,), (1,)), ((), ()))
NN = (((1,), (0,)), ((), ()))
TN = (((0,), (0,)), ((), ()))

T = 8
D = 1792
HALF = D // 2
F = 928
WIDE = 512
CUTS = (slice(0, WIDE), slice(WIDE, F))
ROWS = 8

BLOCKS = (
    (0, 2), (0, -2), (1, 0), (0, 1),
    (0, 4), (0, 3), (0, -3), (1, 2),
    (1, 4), (1, 3), (1, -3), (0, -1),
    (1, -2), (1, 1), (1, -1), (0, 0),
)
ONWARD = {
    (0, 0): ((0, 2), (0, -2), (1, 0), (0, 1), (0, -1)),
    (0, 2): ((1, 0), (0, -1)),
    (0, -2): ((1, 0), (0, 1)),
    (1, 0): ((0, 1), (0, -1)),
    (1, 2): ((0, -1),),
    (1, -2): ((0, 1),),
}
SLOT = {block: i for i, block in enumerate(BLOCKS)}
HOME = SLOT[(0, 0)]
BATCHES = 4
PER = len(BLOCKS) // BATCHES
TB = PER * 2 * T


def dot(a, b, dims):
    return lax.dot_general(a, b, dims, preferred_element_type=F32)


def mirrored(block):
    y, d = block
    return SLOT[(y, d if d == 4 else -d)]


def stack(a, b):
    return jnp.concatenate([a, b], axis=0)


def folded(low, high):
    pad = jnp.zeros((T, 2 * WIDE - F), F32)
    return stack(low, jnp.concatenate([high, pad], axis=1)).astype(BF16)


def unfold(ref, at, one, two):
    ref[at : at + 16, :WIDE] = stack(one[:T], two[:T])
    ref[at : at + 16, WIDE:] = stack(one[T:, : F - WIDE], two[T:, : F - WIDE])


def fetch_wait(ref, sem):
    pltpu.make_async_copy(ref, ref, sem).wait()


def kernel(
    x_in_hbm, x_og_hbm, w_in_hbm, w_out_hbm,
    in_grad, w_in_grad, w_out_grad,
    x, w_in, w_out, w_in_t, w_out_t, mine, sibs, acts, part_low, part_high, part_in_low, part_in_high, act, late, hid, pgr, to_sib, keep, from_sib, comb, comb_in,
    near_sem, far_sem, x_sem, w_sem, mine_sem, sibs_sem, part_sem, act_sem, late_sem, fs_sem, comb_sem,
    mine_out, sibs_out, part_out, act_out, late_out, fs_out, comb_out,
):
    parts, parts_in = (part_low, part_high), (part_in_low, part_in_high)
    r, c = lax.axis_index("row"), lax.axis_index("col")
    y_hi, z, k = c // 16, lax.rem(c // 2, 8), lax.rem(c, 2)

    def chip(y, d):
        return (r, lax.rem(y_hi + y, 2) * 16 + lax.rem(z + d + 8, 8) * 2 + k)

    sibling = (r, c + 1 - 2 * k)

    y_lo, x_at = r // 4, lax.rem(r, 4)
    me = 2 * x_at + y_lo
    y_peer = (lax.rem(r + 4, ROWS), c)

    def peer(j):
        return lax.rem(r + j, ROWS)

    def x_peer(j):
        return (4 * y_lo + lax.rem(x_at + j, 4), c)

    def send(src, dst, out, sem, to):
        pltpu.make_async_remote_copy(
            src_ref=src, dst_ref=dst, send_sem=out, recv_sem=sem, device_id=to, device_id_type=MESH
        ).start()

    weights = [pltpu.make_async_copy(w_in_hbm, w_in, w_sem.at[0]), pltpu.make_async_copy(w_out_hbm, w_out, w_sem.at[1])]
    tokens = [pltpu.make_async_copy(x_in_hbm, x.at[0], x_sem.at[0]), pltpu.make_async_copy(x_og_hbm, x.at[1], x_sem.at[1])]
    barrier = pltpu.get_barrier_semaphore()
    row_friends = [x_peer(1), x_peer(3), y_peer]
    friends = [chip(*block) for block in ONWARD[(0, 0)]] + [sibling] + row_friends
    for friend in friends:
        pl.semaphore_signal(barrier, inc=1, device_id=friend, device_id_type=MESH)
    for copy in tokens + weights:
        copy.start()
    for a in range(2):
        tokens[a].wait()
        block = x[a].astype(F32)
        mine[HOME, a] = stack(block[:, :HALF], block[:, HALF:]).astype(BF16)
    pl.semaphore_wait(barrier, len(friends))

    def forward(block):
        slot = SLOT[block]
        for to in ONWARD.get(block, ()):
            seen = SLOT[((block[0] + to[0]) % 2, block[1] - to[1])]
            send(mine.at[slot], mine.at[seen], mine_out, mine_sem.at[seen], chip(*to))
        if block[1] == -2:
            far, near = SLOT[(block[0], 4)], SLOT[(block[0], 2)]
            send(mine.at[near + k * (slot - near)], mine.at[far], mine_out, mine_sem.at[far], chip(0, 4 * k - 2))
        send(mine.at[slot], sibs.at[slot], sibs_out, sibs_sem.at[slot], sibling)

    def arrive(*blocks):
        for block in blocks:
            slot = SLOT[block]
            fetch_wait(mine.at[slot], mine_sem.at[slot])
            forward(block)

    def unpack(b):
        for s in range(PER * b, PER * b + PER):
            fetch_wait(sibs.at[s], sibs_sem.at[s])
            for a in range(2):
                own, sib = mine[s, a], sibs[s, a]
                acts[a, 16 * s : 16 * s + 16, :HALF] = stack(own[:T], sib[:T])
                acts[a, 16 * s : 16 * s + 16, HALF:] = stack(own[T:], sib[T:])

    def up(b, half):
        rows = slice(TB * b, TB * b + TB)
        pre = dot(acts[0, rows], w_in_t[:, CUTS[half]], NN)
        back = dot(acts[1, rows], w_out_t[:, CUTS[half]], NN)
        part, part_in, sem, out = parts[half], parts_in[half], part_sem.at[half, b], part_out.at[half, b]
        for i in range(ROWS):
            part[b, i // 2, i % 2] = stack(pre[T * i : T * i + T], back[T * i : T * i + T]).astype(BF16)
        for j in range(1, ROWS):
            to = peer(j)
            send(part.at[b, lax.rem(to, 4), to // 4], part_in.at[b, j - 1], out, sem, (to, c))

    def activate(b):
        hidden, grads = [], []
        for half in range(2):
            part, part_in = parts[half], parts_in[half]
            fetch_wait(part_in.at[b], part_sem.at[half, b])
            total = part[b, x_at, y_lo].astype(F32)
            for j in range(ROWS - 1):
                total += part_in[b, j].astype(F32)
            pre, back = total[:T], total[T:]
            cdf = 0.5 * (1.0 + lax.erf(pre * (1.0 / math.sqrt(2.0))))
            slope = cdf + pre * jnp.exp(-0.5 * pre * pre) * (1.0 / math.sqrt(2.0 * math.pi))
            hidden.append(pre * cdf)
            grads.append(back * slope)
        act[b, me] = folded(*grads)
        late[me, b] = folded(*hidden)
        own = act.at[b, me]
        for j in range(1, ROWS):
            send(own, own, act_out.at[b], act_sem.at[b], (peer(j), c))

    def spread_late():
        own = late.at[me]
        for j in range(1, ROWS):
            send(own, own, late_out, late_sem, (peer(j), c))

    def down(b):
        fetch_wait(act.at[b, pl.ds(0, ROWS - 1)], act_sem.at[b])
        for i in range(0, ROWS, 2):
            unfold(pgr, TB * b + T * i, act[b, i], act[b, i + 1])
        grad = dot(pgr[TB * b : TB * b + TB], w_in[...], NN)
        for i in range(PER):
            own, sib = grad[16 * i : 16 * i + T], grad[16 * i + T : 16 * i + 16]
            to_sib[b, i] = stack(sib[:, :HALF], sib[:, HALF:]).astype(BF16)
            keep[b, i] = stack(own[:, :HALF], own[:, HALF:])
        send(to_sib.at[b], from_sib.at[b], fs_out.at[b], fs_sem.at[b], sibling)

    def combine(b):
        fetch_wait(from_sib.at[b], fs_sem.at[b])
        for i in range(PER):
            s = PER * b + i
            total = keep[b, i] + from_sib[b, i].astype(F32)
            if s == HOME:
                keep[b, i] = total
            else:
                comb[s] = total.astype(BF16)
                seen = mirrored(BLOCKS[s])
                send(comb.at[s], comb_in.at[seen], comb_out, comb_sem.at[seen], chip(*BLOCKS[s]))

    forward((0, 0))
    for friend in row_friends:
        pl.semaphore_signal(near_sem, inc=1, device_id=friend, device_id_type=MESH)
    weights[0].wait()
    w_in_t[...] = w_in[...].T
    weights[1].wait()
    w_out_t[...] = w_out[...].T
    pl.semaphore_wait(near_sem, len(row_friends))
    pl.semaphore_signal(far_sem, inc=1, device_id=x_peer(1), device_id_type=MESH)
    arrive((0, 2), (0, -2), (1, 0), (0, 1), (0, -1))
    pl.semaphore_wait(far_sem, 1)
    unpack(0)
    up(0, 0)
    up(0, 1)
    arrive((0, 3), (0, -3), (1, 2), (1, -2), (0, 4), (1, 1), (1, -1))
    unpack(1)
    up(1, 0)
    up(1, 1)
    unpack(3)
    arrive((1, 3), (1, -3))
    up(3, 0)
    arrive((1, 4))
    up(3, 1)
    unpack(2)
    up(2, 0)
    up(2, 1)
    activate(0)
    activate(1)
    activate(2)
    down(0)
    activate(3)
    spread_late()
    combine(0)
    down(1)
    down(2)
    combine(1)
    combine(2)
    down(3)
    combine(3)
    w_in_grad[...] = dot(pgr[...], acts[0], TN).astype(BF16)
    fetch_wait(late.at[pl.ds(0, ROWS - 1)], late_sem)
    for b in range(BATCHES):
        for i in range(0, ROWS, 2):
            unfold(hid, TB * b + T * i, late[i, b], late[i + 1, b])
    w_out_grad[...] = dot(hid[...], acts[1], TN).astype(BF16)
    total = keep[HOME // PER, HOME % PER]
    for s in range(len(BLOCKS)):
        if s == HOME:
            continue
        fetch_wait(comb_in.at[s], comb_sem.at[s])
        total += comb_in[s].astype(F32)
    in_grad[:, :HALF] = total[:T].astype(BF16)
    in_grad[:, HALF:] = total[T:].astype(BF16)

    fetch_wait(mine.at[pl.ds(0, len(BLOCKS) - 1)], mine_out)
    fetch_wait(sibs, sibs_out)
    fetch_wait(late.at[pl.ds(0, ROWS - 1)], late_out)
    fetch_wait(comb.at[pl.ds(0, len(BLOCKS) - 1)], comb_out)
    for b in range(BATCHES):
        for half in range(2):
            fetch_wait(parts_in[half].at[b], part_out.at[half, b])
        fetch_wait(act.at[b, pl.ds(0, ROWS - 1)], act_out.at[b])
        fetch_wait(to_sib.at[b], fs_out.at[b])


PIECES = 2


def flush(x, gi, go, x_hbm, gi_hbm, go_hbm, sem):
    copies = [pltpu.make_async_copy(x, x_hbm, sem.at[2 * PIECES])]
    n = F // PIECES
    for i in range(PIECES):
        at = pl.ds(n * i, n)
        copies.append(pltpu.make_async_copy(gi.at[at], gi_hbm.at[at], sem.at[2 * i]))
        copies.append(pltpu.make_async_copy(go.at[at], go_hbm.at[at], sem.at[2 * i + 1]))
    for copy in copies:
        copy.start()
    for copy in copies:
        copy.wait()


def on_device(inputs, out_grad, w_in, w_out):
    vmem = pl.BlockSpec(memory_space=pltpu.VMEM)
    hbm = pl.BlockSpec(memory_space=pl.ANY)
    n = len(BLOCKS)
    dma = pltpu.SemaphoreType.DMA
    outs = pl.pallas_call(
        kernel,
        out_shape=(pltpu.VMEM((T, D), BF16), pltpu.VMEM((F, D), BF16), pltpu.VMEM((F, D), BF16)),
        in_specs=[hbm] * 4,
        out_specs=(vmem, vmem, vmem),
        scratch_shapes=[
            pltpu.VMEM((2, T, D), BF16),
            pltpu.VMEM((F, D), BF16),
            pltpu.VMEM((F, D), BF16),
            pltpu.VMEM((D, F), BF16),
            pltpu.VMEM((D, F), BF16),
            pltpu.VMEM((n, 2, 16, HALF), BF16),
            pltpu.VMEM((n, 2, 16, HALF), BF16),
            pltpu.VMEM((2, 16 * n, D), BF16),
            pltpu.VMEM((BATCHES, 4, 2, 16, WIDE), BF16),
            pltpu.VMEM((BATCHES, 4, 2, 16, F - WIDE), BF16),
            pltpu.VMEM((BATCHES, ROWS - 1, 16, WIDE), BF16),
            pltpu.VMEM((BATCHES, ROWS - 1, 16, F - WIDE), BF16),
            pltpu.VMEM((BATCHES, ROWS, 16, WIDE), BF16),
            pltpu.VMEM((ROWS, BATCHES, 16, WIDE), BF16),
            pltpu.VMEM((16 * n, F), BF16),
            pltpu.VMEM((16 * n, F), BF16),
            pltpu.VMEM((BATCHES, PER, 16, HALF), BF16),
            pltpu.VMEM((BATCHES, PER, 16, HALF), F32),
            pltpu.VMEM((BATCHES, PER, 16, HALF), BF16),
            pltpu.VMEM((n, 16, HALF), BF16),
            pltpu.VMEM((n, 16, HALF), BF16),
            pltpu.SemaphoreType.REGULAR,
            pltpu.SemaphoreType.REGULAR,
            dma((2,)),
            dma((2,)),
            dma((n,)),
            dma((n,)),
            dma((2, BATCHES)),
            dma((BATCHES,)),
            dma,
            dma((BATCHES,)),
            dma((n,)),
            dma,
            dma,
            dma((2, BATCHES)),
            dma((BATCHES,)),
            dma,
            dma((BATCHES,)),
            dma,
        ],
        compiler_params=pltpu.CompilerParams(collective_id=0, has_side_effects=True, vmem_limit_bytes=44 << 20),
        name="block",
    )(*(pltpu.with_memory_space_constraint(a, pltpu.HBM) for a in (inputs, out_grad, w_in.T, w_out)))
    in_grad, w_in_grad, w_out_grad = pl.pallas_call(
        flush,
        out_shape=tuple(jax.ShapeDtypeStruct(o.shape, BF16) for o in outs),
        in_specs=[vmem] * 3,
        out_specs=(hbm,) * 3,
        scratch_shapes=[dma((2 * PIECES + 1,))],
        compiler_params=pltpu.CompilerParams(vmem_limit_bytes=16 << 20),
        name="flush",
    )(*outs)
    return (in_grad, w_in_grad.T, w_out_grad)


def solution(mesh):
    placed = (P("col", "row"), P("col", "row"), P("row", "col"), P("col", "row"))
    return jax.shard_map(
        on_device,
        mesh=mesh,
        in_specs=placed,
        out_specs=(P("col", "row"), P("row", "col"), P("col", "row")),
        check_vma=False,
    )
```

time: 56.1 us -> 55.2 us (0.984)
  no operation moved by 1% of the time
where the time goes in v3:
time: 55.2 us; the launch traced here: 55.1 us
  Pallas kernels  54.5 us (99%)
  between operations  0.64 us (1%)
    pallas_call x1, Pallas kernels, on_device(): pl.pallas_call(kernel, out_shape=(pltpu.VMEM((T, D), BF16), pltpu.VMEM((F...  51.6 us
    pallas_call x1, Pallas kernels, on_device(): pl.pallas_call(flush, out_shape=tuple((jax.ShapeDtypeStruct(o.shape, BF16...  2.87 us

profile of v3, /device:TPU:1, one launch (start us, length us, event | category | flops | bytes accessed | tf_op | source)
XLA Modules:
  0.0 55.1 jit_solution(2527925829875018543)
XLA Ops:
  0.6 51.6 %block.1 = (bf16[8,1792]{1,0:T(8,128)(2,1)S(1)}, bf16[928,1792]{1,0:T(8,128)(2,1)S(1)}, bf16[928,1792]{1,0:T(8,128)(2,1)S(1)}) custom-call(bf16[8,1792]{1,0:T(8,128)(2,1)} %x_in_hbm.1, bf16[8,1792]{1,0:T(8,128)(2,1)} %x_og_hbm.1, bf16[928,1792]{1,0:T(8,128)(2,1)} %bitcast.2, bf16[928,1792]{1,0:T(8,128)(2,1)} %w_out_hbm.1), custom_call_target="tpu_custom_call" | custom-call | tf_op jit(solution)/shard_map/block/pallas_call | solution.py:287
  52.2 2.9 %flush.1 = (bf16[8,1792]{1,0:T(8,128)(2,1)}, bf16[928,1792]{1,0:T(8,128)(2,1)}, bf16[928,1792]{1,0:T(8,128)(2,1)}) custom-call(bf16[8,1792]{1,0:T(8,128)(2,1)S(1)} %get-tuple-element.9.x, bf16[928,1792]{1,0:T(8,128)(2,1)S(1)} %get-tuple-element.10.gi, bf16[928,1792]{1,0:T(8,128)(2,1)S(1)} %get-tuple-element.11.go), custom_call_target="tpu_custom_call" | custom-call | tf_op jit(solution)/shard_map/flush/pallas_call | solution.py:336

commit v4 on v3

--- a/solution.py
+++ b/solution.py
@@ -108,12 +108,14 @@
     friends = [chip(*block) for block in ONWARD[(0, 0)]] + [sibling] + row_friends
     for friend in friends:
         pl.semaphore_signal(barrier, inc=1, device_id=friend, device_id_type=MESH)
-    for copy in tokens + weights:
+    for copy in tokens:
         copy.start()
     for a in range(2):
         tokens[a].wait()
         block = x[a].astype(F32)
         mine[HOME, a] = stack(block[:, :HALF], block[:, HALF:]).astype(BF16)
+    for copy in weights:
+        copy.start()
     pl.semaphore_wait(barrier, len(friends))
 
     def forward(block):
@@ -226,17 +228,17 @@
     up(2, 1)
     activate(0)
     activate(1)
+    activate(3)
+    down(0)
     activate(2)
-    down(0)
-    activate(3)
     spread_late()
     combine(0)
     down(1)
+    down(3)
+    combine(1)
+    combine(3)
     down(2)
-    combine(1)
     combine(2)
-    down(3)
-    combine(3)
     w_in_grad[...] = dot(pgr[...], acts[0], TN).astype(BF16)
     fetch_wait(late.at[pl.ds(0, ROWS - 1)], late_sem)
     for b in range(BATCHES):

time: 55.2 us -> 56.2 us (1.018)
  Pallas kernels: 54.5 us -> 55.4 us
    pallas_call x1, Pallas kernels: 51.6 us -> 52.5 us  [on_device(): pl.pallas_call(kernel, out_shape=(pltpu.VMEM((T, D), BF16), pltpu.VMEM((F...]
where the time goes in v4:
time: 56.2 us; the launch traced here: 56 us
  Pallas kernels  55.4 us (99%)
  between operations  0.64 us (1%)
    pallas_call x1, Pallas kernels, on_device(): pl.pallas_call(kernel, out_shape=(pltpu.VMEM((T, D), BF16), pltpu.VMEM((F...  52.5 us
    pallas_call x1, Pallas kernels, on_device(): pl.pallas_call(flush, out_shape=tuple((jax.ShapeDtypeStruct(o.shape, BF16...  2.87 us

profile of v4, /device:TPU:1, one launch (start us, length us, event | category | flops | bytes accessed | tf_op | source)
XLA Modules:
  0.0 56.0 jit_solution(34791361906902947)
XLA Ops:
  0.6 52.5 %block.1 = (bf16[8,1792]{1,0:T(8,128)(2,1)S(1)}, bf16[928,1792]{1,0:T(8,128)(2,1)S(1)}, bf16[928,1792]{1,0:T(8,128)(2,1)S(1)}) custom-call(bf16[8,1792]{1,0:T(8,128)(2,1)} %x_in_hbm.1, bf16[8,1792]{1,0:T(8,128)(2,1)} %x_og_hbm.1, bf16[928,1792]{1,0:T(8,128)(2,1)} %bitcast.2, bf16[928,1792]{1,0:T(8,128)(2,1)} %w_out_hbm.1), custom_call_target="tpu_custom_call" | custom-call | tf_op jit(solution)/shard_map/block/pallas_call | solution.py:289
  53.2 2.9 %flush.1 = (bf16[8,1792]{1,0:T(8,128)(2,1)}, bf16[928,1792]{1,0:T(8,128)(2,1)}, bf16[928,1792]{1,0:T(8,128)(2,1)}) custom-call(bf16[8,1792]{1,0:T(8,128)(2,1)S(1)} %get-tuple-element.9.x, bf16[928,1792]{1,0:T(8,128)(2,1)S(1)} %get-tuple-element.10.gi, bf16[928,1792]{1,0:T(8,128)(2,1)S(1)} %get-tuple-element.11.go), custom_call_target="tpu_custom_call" | custom-call | tf_op jit(solution)/shard_map/flush/pallas_call | solution.py:338
